TPU v7x, 256 devices: a whole 4x4x8 slice. The times are simulated.
256 devices in a mesh: dp: 32 (over x, y, core), tensor: 8 (over z).
Axes of the slice: x: 4, y: 4, z: 8, core: 2. Of those that a mesh axis runs over, the one named last changes fastest.
Arguments:
- activations: bfloat16 [16384, 18432], P('dp', 'tensor'), may hold values from -36 to 36
- out_grad: bfloat16 [16384, 2304], P(('dp', 'tensor')), may hold values from -1.08 to 1.08
- accum: float32 [18432, 2304], P(('tensor', 'dp')), may hold values from -6 to 6
- noise: float32 [18432, 2304], P(('tensor', 'dp')), may hold values from -6 to 6
Outputs:
- noisy_sum: float32 [18432, 2304], P(('tensor', 'dp'))
- clip_factors: float32 [32], P('dp')
All inputs are finite; a program needn't handle non-finite values.
Results may differ from a plain program's by a relative error of at most 0.0003.
Values may be sent and summed in bfloat16 or wider, within the bound.
A program may use at most 128 MiB of HBM per device.

v0:
```python
import math

import jax
import jax.numpy as jnp
from jax import lax
from jax.sharding import PartitionSpec as P


def clip_factor(partial_value, bound):
    sq_norm = lax.psum(partial_value, "tensor")
    return jnp.minimum(1.0, bound / jnp.sqrt(sq_norm))


def local(activations, out_grad, accum, noise):
    length = activations.shape[0]
    hidden_all = activations.shape[1] * lax.axis_size("tensor")
    width = out_grad.shape[1]
    bound = 0.02 * math.sqrt(length * hidden_all * width)
    upstream = lax.all_gather(out_grad, "tensor", axis=0, tiled=True)
    act_gram = jnp.einsum("tf,sf->ts", activations, activations, preferred_element_type=jnp.float32)
    out_gram = jnp.einsum("td,sd->ts", upstream, upstream, preferred_element_type=jnp.float32)
    partial_value = jnp.sum(act_gram * out_gram)
    factor = clip_factor(partial_value, bound)
    total = lax.psum_scatter(
        factor * jnp.einsum("tf,td->fd", activations, upstream, preferred_element_type=jnp.float32),
        "dp",
        scatter_dimension=0,
        tiled=True,
    )
    return (accum + total + noise, jnp.reshape(factor, (1,)))


def solution(mesh):
    in_specs = (
        P("dp", "tensor"),
        P(("dp", "tensor"), None),
        P(("tensor", "dp"), None),
        P(("tensor", "dp"), None),
    )
    out_specs = (P(("tensor", "dp"), None), P("dp"))
    return jax.shard_map(local, mesh=mesh, in_specs=in_specs, out_specs=out_specs, check_vma=False)
```

profile of v0, /device:TPU:1, one launch (start us, length us, event | category | flops | bytes accessed | tf_op | source)
XLA Modules:
  0.0 234.3 jit_solution(14215339229425986795)
XLA Ops:
  7.2 0.0 copy-start
  7.2 0.0 all-gather.2.cloned.1.call-start
  7.2 0.7 all-gather.2.cloned.1.call-update
  7.9 0.0 reduce-scatter.2.cloned.1.call-start
  8.0 0.9 copy-done
  8.8 1.4 fusion.1
  10.2 42.0 %all-gather.2.cloned.1.call-done = bf16[512,2304]{1,0:T(8,128)(2,1)} async-done(((bf16[64,2304]{1,0:T(8,128)(2,1)}), bf16[512,2304]{1,0:T(8,128)(2,1)}) %all-gather.2.cloned.1.call-update) | async-done | bytes 2359312 | tf_op jit(solution)/shard_map/all_gather | solution.py:19
  52.3 4.5 %fusion = f32[]{:T(128)} fusion(f32[512,512]{1,0:T(8,128)S(1)} %fusion.1, bf16[512,2304]{1,0:T(8,128)(2,1)} %all-gather.2.cloned.1.call-done), kind=kOutput, calls=%fused_computation.2 | convolution fusion | flops 1208483840 | bytes 3407876 | tf_op jit(solution)/shard_map/td,sd->ts/dot_general | solution.py:21
  56.8 13.1 %psum.7 = f32[]{:T(128)} all-reduce(f32[]{:T(128)} %fusion), channel_id=1, replica_groups=mesh['dp'=32,'tensor'=8] {'tensor'}, use_global_device_ids=true, to_apply=%region_1.0 | all-reduce | flops 1 | bytes 8 | tf_op jit(solution)/shard_map/psum | solution.py:10
  70.5 11.7 %convolution_multiply_fusion = f32[2304,2304]{1,0:T(8,128)} fusion(bf16[512,2304]{1,0:T(8,128)(2,1)S(1)} %copy-done, bf16[512,2304]{1,0:T(8,128)(2,1)} %all-gather.2.cloned.1.call-done, f32[]{:T(128)} %min_shard_map.3), kind=kOutput, calls=%fused_computation | convolution fusion | flops 5441126400 | bytes 25952260 | tf_op jit(solution)/shard_map/tf,td->fd/dot_general | solution.py:25
  82.2 0.0 copy-start.1
  82.2 0.0 reduce-scatter.2.cloned.1.call-update
  82.3 141.8 %reduce-scatter.2.cloned.1.call-done = f32[72,2304]{1,0:T(8,128)} async-done(((f32[2304,2304]{1,0:T(8,128)}), f32[72,2304]{1,0:T(8,128)}) %reduce-scatter.2.cloned.1.call-update) | async-done | bytes 663568 | tf_op jit(solution)/shard_map/reduce_scatter | solution.py:24
  224.1 0.0 copy-done.1
  224.1 2.2 add_add_fusion
Async XLA Ops:
  7.2 1.7 copy-start
  7.2 45.1 %all-gather.2.cloned.1.call-start = ((), (), s32[]{:S(2)}) async-start(), calls=%async_computation.1 | async-start | bytes 2654208 | tf_op jit(solution)/shard_map/all_gather | solution.py:19
  7.9 216.1 %reduce-scatter.2.cloned.1.call-start = ((), (), s32[]{:S(2)}) async-start(), calls=%async_computation.2 | async-start | bytes 21897216 | tf_op jit(solution)/shard_map/reduce_scatter | solution.py:24
  82.2 141.8 %copy-start.1 = (f32[72,2304]{1,0:T(8,128)S(1)}, f32[72,2304]{1,0:T(8,128)}, u32[]{:S(2)}) copy-start(f32[72,2304]{1,0:T(8,128)} %param.7) | copy-start | bytes 1990660
Sparse Core Ops, SparseCore 0:
  9.8 42.4 all-gather.1
  82.4 141.6 reduce-scatter.1
where the time goes:
time: 234 us
  waiting for transfers between devices  185 us (79%)
  matrix products  17.6 us (8%)
  between operations  15.9 us (7%)
  blocking collectives  13.1 us (6%)
    reduce_scatter x1, waiting for transfers between devices, local(): lax.psum_scatter(factor * jnp.einsum('tf,td->fd', activations, upstream,...  142 us
    all_gather x1, waiting for transfers between devices, local(): upstream = lax.all_gather(out_grad, 'tensor', axis=0, tiled=True)  42 us
    psum x1, blocking collectives, clip_factor(): sq_norm = lax.psum(partial_value, 'tensor')  13.1 us
    dot_general x1, matrix products, local(): jnp.einsum('tf,td->fd', activations, upstream, preferred_element_type=jnp...  11.7 us
  transfers between devices with their start and end apart: 2, of which 2 were waited for; matrix products, arithmetic and copies ran while one was open for 1% of the time, Pallas kernels for 0%

commit v1 on v0

v1 whole, which is shorter than its diff:
```python
import functools
import math

import jax
import jax.numpy as jnp
from jax import lax
from jax.experimental import pallas as pl
from jax.experimental.pallas import tpu as pltpu
from jax.sharding import PartitionSpec as P

MESH = pl.DeviceIdType.MESH
LEN = 512
FF = 2304
D = 2304
HALF = D // 2
ROWS = 64
SUB = 16
NSUB = ROWS // SUB
CHUNK = 144
WIDTH = (640, 512)
START = (0, 640)
STEP = 48
TOP = 80

SLOT = ((0, 1, 3, 5, 7), (0, 2, 4, 6, 7))
SUBS = ((0, 1, 2, 3), (2, 3, 0, 1))
BLOCK = (0, -1, 1, -2, 2, -3, 3, 4)
GATHER = 3 * NSUB + NSUB // 2

ORDER = ((2, 3, 1, 0, 2, 3), (1, 0, 2, 3, 1, 0))

POWER = 9
REACH = 2.0**14


def encode(x, scale):
    y = x * scale
    y2 = y * y
    y4 = y2 * y2
    return (y4 * y4 * y).astype(jnp.bfloat16)


def decode(sent, unscale):
    z = sent.astype(jnp.float32)
    r = jnp.exp(jnp.log(jnp.abs(z)) * (1.0 / POWER)) * unscale
    return jnp.where(z < 0, -r, r)


def fold(prod):
    total = None
    for i in range(0, prod.shape[0], 8):
        for j in range(0, prod.shape[1], 128):
            piece = prod[i : i + 8, j : j + 128]
            total = piece if total is None else total + piece
    return total


def kernel(
    bound, h_hbm, g_hbm, acc_hbm, noise_hbm, out_ref, clip_ref,
    hs, hp, ht, gs, gp, t, gram, norm, norms, send0, send1, recv0, recv1, sum0, sum1, fin, swap, acc, noise,
    load_sem, gs_send, gs_recv, hp_send, hp_recv, gp_send, gp_recv, n_send, n_recv, rs_send, rs_recv, swap_sem,
):
    dp, z = lax.axis_index("dp"), lax.axis_index("tensor")
    x, y, c = dp // 8, (dp // 2) % 4, dp % 2
    o = 1 - c
    partner = (dp - c + o, z)
    along_z = ((dp, (z + 1) % 8), (dp, (z + 7) % 8))
    sends, recvs, sums = (send0, send1), (recv0, recv1), (sum0, sum1)

    ia = (x * o + y * c, y * o + x * c)
    ib = (ia[1], ia[0])
    step_a = (4 * o + c, o + 4 * c)
    step_b = (step_a[1], step_a[0])

    def chunk_of(part, a, b):
        return ((ia[part] + a + 4) % 4) * step_a[part] + ((ib[part] + b + 4) % 4) * step_b[part]

    def device_of(part, a, b):
        return (chunk_of(part, a, b) * 2 + c, z)

    loads = []
    for s in range(8):
        row = pl.multiple_of(((z + BLOCK[s] + 8) % 8) * ROWS, ROWS)
        loads.append(pltpu.make_async_copy(h_hbm.at[pl.ds(row, ROWS)], hs.at[pl.ds(s * ROWS, ROWS)], load_sem.at[s]))
    g_load = pltpu.make_async_copy(g_hbm, gs.at[pl.ds(0, ROWS)], load_sem.at[8])
    acc_load = pltpu.make_async_copy(acc_hbm, acc, load_sem.at[9])
    noise_load = pltpu.make_async_copy(noise_hbm, noise, load_sem.at[10])
    g_load.start()
    for copy in loads:
        copy.start()
    acc_load.start()
    noise_load.start()

    others = [(dp, (z + k) % 8) for k in range(1, 8)]
    others += [(partner[0], (z + k) % 8) for k in range(8)]
    others += [device_of(0, 1, 0), device_of(0, -1, 0), device_of(0, 0, 1), device_of(0, 0, -1)]
    barrier = pltpu.get_barrier_semaphore()
    for device in others:
        pl.semaphore_signal(barrier, inc=1, device_id=device, device_id_type=MESH)
    pl.semaphore_wait(barrier, len(others))

    def gather(way, n):
        sub = SUBS[way][n % NSUB]
        src = gs.at[pl.ds(SLOT[way][n // NSUB] * ROWS + sub * SUB, SUB)]
        dst = gs.at[pl.ds(SLOT[way][n // NSUB + 1] * ROWS + sub * SUB, SUB)]
        return pltpu.make_async_remote_copy(
            src_ref=src, dst_ref=dst, send_sem=gs_send.at[way, n], recv_sem=gs_recv.at[way, n],
            device_id=along_z[way], device_id_type=MESH,
        )

    def give_h(s):
        return pltpu.make_async_remote_copy(
            src_ref=hs.at[pl.ds(s * ROWS, ROWS)], dst_ref=hp.at[pl.ds(s * ROWS, ROWS)],
            send_sem=hp_send.at[s], recv_sem=hp_recv.at[s], device_id=partner, device_id_type=MESH,
        )

    mine = pl.ds(pl.multiple_of(c * HALF, 128), HALF)
    theirs = pl.ds(pl.multiple_of(o * HALF, 128), HALF)

    def give_g(s):
        return pltpu.make_async_remote_copy(
            src_ref=gs.at[pl.ds(s * ROWS, ROWS), theirs], dst_ref=gp.at[pl.ds(s * ROWS, ROWS)],
            send_sem=gp_send.at[s], recv_sem=gp_recv.at[s], device_id=partner, device_id_type=MESH,
        )

    g_load.wait()
    for n in range(NSUB):
        for way in range(2):
            gather(way, n).start()
    give_g(0).start()
    for s in range(8):
        loads[s].wait()
        give_h(s).start()

    def act_gram(i, _):
        r = pl.ds(pl.multiple_of(i * 128, 128), 128)
        gram[r, :] = lax.dot_general(
            hs[r, :], hs[...], (((1,), (1,)), ((), ())), preferred_element_type=jnp.float32
        )
        return 0

    def transpose(src, e):
        def body(i, _):
            r = pl.ds(pl.multiple_of(i * 128, 128), 128)
            ht[e, r, :] = src[:, r].T
            return 0

        lax.fori_loop(0, FF // 128, body, 0)

    def out_gram(lo, hi):
        prod = gram[lo:hi, 0:hi] * lax.dot_general(
            gs[lo:hi, :], gs[0:hi, :], (((1,), (1,)), ((), ())), preferred_element_type=jnp.float32
        )
        total = fold(prod[:, lo:hi])
        return total if lo == 0 else total + 2.0 * fold(prod[:, 0:lo])

    def terms(e, lo, first):
        def body(i, _):
            r = pl.ds(pl.multiple_of(i * 256, 256), 256)
            rhs = gs[lo : lo + 256, mine] if e == 0 else gp[lo : lo + 256, :]
            value = jnp.dot(ht[e, r, lo : lo + 256], rhs, preferred_element_type=jnp.float32)
            if first:
                t[e, r, :] = value
            else:
                t[e, r, :] += value
            return 0

        lax.fori_loop(0, FF // 256, body, 0)

    for n in range(GATHER):
        for way in range(2):
            gather(way, n).wait_recv()
            if n + NSUB < GATHER:
                gather(way, n + NSUB).start()
        if n % NSUB == NSUB - 1:
            for way in range(2):
                give_g(SLOT[way][n // NSUB + 1]).start()
        if n == 0:
            lax.fori_loop(0, 4, act_gram, 0)
        elif n == 1:
            transpose(hs, 0)
        elif n == 3:
            for s in range(8):
                give_h(s).wait_recv()
            transpose(hp, 1)
        elif n == 8:
            norm[...] = out_gram(0, 256)
            terms(0, 0, True)
        elif n == 9:
            for s in range(4):
                give_g(s).wait_recv()
            terms(1, 0, True)
        elif n == 11:
            norm[...] += out_gram(256, 384)
    give_g(7).start()

    norm[...] += out_gram(384, 512)

    def give_norm(e, k):
        device = (dp if e == 0 else partner[0], (z + k) % 8)
        return pltpu.make_async_remote_copy(
            src_ref=norm, dst_ref=norms.at[e, k], send_sem=n_send.at[e, k], recv_sem=n_recv.at[e, k],
            device_id=device, device_id_type=MESH,
        )

    pairs = [(e, k) for k in (4, 3, 5, 2, 6, 1, 7, 0) for e in range(2) if (e, k) != (0, 0)]
    for e, k in pairs:
        give_norm(e, k).start()
    terms(0, 256, False)
    for s in range(4, 8):
        give_g(s).wait_recv()
    terms(1, 256, False)
    for e, k in pairs:
        give_norm(e, k).wait_recv()

    def factor(e):
        total = norm[...] if e == 0 else norms[1, 0]
        for k in range(1, 8):
            total = total + norms[e, k]
        sq_norm = jnp.broadcast_to(jnp.sum(total), (8, 128))
        return jnp.max(jnp.minimum(1.0, bound / jnp.sqrt(sq_norm)))

    f0, f1 = factor(0), factor(1)
    clip_ref[0] = f0

    limit = 2.0 * bound
    scale = [REACH / (limit * chips) for chips in (1, 1, 2, 2, 2, 2, 4, 8)]

    def own(part, chunk, r):
        rows = pl.ds(pl.multiple_of(chunk * CHUNK + r, 16), STEP)
        cols = slice(START[part], START[part] + WIDTH[part])
        return f0 * t[0, rows, cols] + f1 * t[1, rows, cols]

    def over_rows(body):
        def step(i, _):
            r = pl.multiple_of(i * STEP, 16)
            body(r, pl.ds(r, STEP))
            return 0

        lax.fori_loop(0, CHUNK // STEP, step, 0)

    def message(part, way, slot):
        sign = 1 - 2 * way
        rows = pl.ds(0, CHUNK)
        if slot == 6:
            rows = pl.ds(0, TOP) if way == 0 else pl.ds(TOP, CHUNK - TOP)
        device = device_of(part, sign, 0) if slot < 6 else device_of(part, 0, sign)
        return pltpu.make_async_remote_copy(
            src_ref=sends[part].at[way, slot, rows], dst_ref=recvs[part].at[way, slot, rows],
            send_sem=rs_send.at[part, way, slot], recv_sem=rs_recv.at[part, way, slot],
            device_id=device, device_id_type=MESH,
        )

    def first_phase(part, way, slot):
        sign = 1 - 2 * way
        chunk = chunk_of(part, 2 if slot < 2 else sign, ORDER[way][slot])
        if slot >= 4:
            message(part, way, slot - 4).wait_recv()

        def body(r, rows):
            value = own(part, chunk, r)
            if slot >= 4:
                value += decode(recvs[part][way, slot - 4, rows, :], 1.0 / scale[slot - 4])
            sends[part][way, slot, rows, :] = encode(value, scale[slot])

        over_rows(body)
        message(part, way, slot).start()

    def take(part, way, slot):
        b = ORDER[way][slot]
        message(part, way, slot).wait_recv()

        def body(r, rows):
            sums[part][b, rows, :] += decode(recvs[part][way, slot, rows, :], 1.0 / scale[slot])

        over_rows(body)

    for slot in range(4):
        for way in range(2):
            for part in range(2):
                first_phase(part, way, slot)
    for part in range(2):
        for b in range(4):
            chunk = chunk_of(part, 0, b)

            def body(r, rows):
                sums[part][b, rows, :] = own(part, chunk, r)

            over_rows(body)
    for slot in (4, 5):
        for way in range(2):
            for part in range(2):
                first_phase(part, way, slot)
    for slot in (2, 3, 4):
        for way in range(2):
            for part in range(2):
                take(part, way, slot)

    for part in range(2):

        def body(r, rows):
            value = encode(sums[part][2, rows, :], scale[6])
            for way in range(2):
                sends[part][way, 6, rows, :] = value

        over_rows(body)
        for way in range(2):
            message(part, way, 6).start()

    def pass_on(part, way):
        b = 1 if way == 0 else 3
        rows = slice(0, TOP) if way == 0 else slice(TOP, CHUNK)
        message(part, way, 6).wait_recv()
        sums[part][b, rows, :] += decode(recvs[part][way, 6, rows, :], 1.0 / scale[6])

        def body(r, rows):
            sends[part][way, 7, rows, :] = encode(sums[part][b, rows, :], scale[7])

        over_rows(body)
        message(part, way, 7).start()

    for part in range(2):
        pass_on(part, 0)
    for way in range(2):
        for part in range(2):
            take(part, way, 5)
    for part in range(2):
        pass_on(part, 1)
    for part in range(2):
        for way in range(2):
            message(part, way, 7).wait_recv()
        cols = slice(START[part], START[part] + WIDTH[part])

        def body(r, rows):
            fin[rows, cols] = (
                sums[part][0, rows, :]
                + decode(recvs[part][0, 7, rows, :], 1.0 / scale[7])
                + decode(recvs[part][1, 7, rows, :], 1.0 / scale[7])
            )

        over_rows(body)

    my_rows = pl.ds(pl.multiple_of(c * (CHUNK // 2), 8), CHUNK // 2)
    their_rows = pl.ds(pl.multiple_of(o * (CHUNK // 2), 8), CHUNK // 2)
    exchange = pltpu.make_async_remote_copy(
        src_ref=fin.at[their_rows], dst_ref=swap, send_sem=swap_sem.at[0], recv_sem=swap_sem.at[1],
        device_id=partner, device_id_type=MESH,
    )
    exchange.start()
    acc_load.wait()
    noise_load.wait()
    out_ref[:, mine] = acc[:, mine] + fin[my_rows, :] + noise[:, mine]
    exchange.wait_recv()
    out_ref[:, theirs] = acc[:, theirs] + swap[...] + noise[:, theirs]

    exchange.wait_send()
    for way in range(2):
        for n in range(GATHER):
            gather(way, n).wait_send()
    for s in range(8):
        give_h(s).wait_send()
        give_g(s).wait_send()
    for e, k in pairs:
        give_norm(e, k).wait_send()
    for part in range(2):
        for way in range(2):
            for slot in range(8):
                message(part, way, slot).wait_send()


def local(activations, out_grad, accum, noise):
    hidden_all = activations.shape[1] * lax.axis_size("tensor")
    bound = 0.02 * math.sqrt(activations.shape[0] * hidden_all * out_grad.shape[1])
    f32, bf16, dma = jnp.float32, jnp.bfloat16, pltpu.SemaphoreType.DMA
    hbm = pl.BlockSpec(memory_space=pl.ANY)
    return pl.pallas_call(
        functools.partial(kernel, bound),
        out_shape=(jax.ShapeDtypeStruct(accum.shape, f32), jax.ShapeDtypeStruct((1,), f32)),
        in_specs=[hbm] * 4,
        out_specs=(pl.BlockSpec(memory_space=pltpu.VMEM), pl.BlockSpec(memory_space=pltpu.SMEM)),
        scratch_shapes=[
            pltpu.VMEM((LEN, FF), bf16),
            pltpu.VMEM((LEN, FF), bf16),
            pltpu.VMEM((2, FF, LEN), bf16),
            pltpu.VMEM((LEN, D), bf16),
            pltpu.VMEM((LEN, HALF), bf16),
            pltpu.VMEM((2, FF, HALF), f32),
            pltpu.VMEM((LEN, LEN), f32),
            pltpu.VMEM((8, 128), f32),
            pltpu.VMEM((2, 8, 8, 128), f32),
            pltpu.VMEM((2, 8, CHUNK, WIDTH[0]), bf16),
            pltpu.VMEM((2, 8, CHUNK, WIDTH[1]), bf16),
            pltpu.VMEM((2, 8, CHUNK, WIDTH[0]), bf16),
            pltpu.VMEM((2, 8, CHUNK, WIDTH[1]), bf16),
            pltpu.VMEM((4, CHUNK, WIDTH[0]), f32),
            pltpu.VMEM((4, CHUNK, WIDTH[1]), f32),
            pltpu.VMEM((CHUNK, HALF), f32),
            pltpu.VMEM((CHUNK // 2, HALF), f32),
            pltpu.VMEM(accum.shape, f32),
            pltpu.VMEM(accum.shape, f32),
            dma((11,)),
            dma((2, GATHER)),
            dma((2, GATHER)),
            dma((8,)),
            dma((8,)),
            dma((8,)),
            dma((8,)),
            dma((2, 8)),
            dma((2, 8)),
            dma((2, 2, 8)),
            dma((2, 2, 8)),
            dma((2,)),
        ],
        compiler_params=pltpu.CompilerParams(
            collective_id=0, has_side_effects=True, vmem_limit_bytes=62 * 2**20
        ),
    )(activations, out_grad, accum, noise)


def solution(mesh):
    in_specs = (
        P("dp", "tensor"),
        P(("dp", "tensor"), None),
        P(("tensor", "dp"), None),
        P(("tensor", "dp"), None),
    )
    out_specs = (P(("tensor", "dp"), None), P("dp"))
    return jax.shard_map(local, mesh=mesh, in_specs=in_specs, out_specs=out_specs, check_vma=False)
```

time: 234 us -> 83.4 us (0.36)
  waiting for transfers between devices: 185 us -> 0 us
  Pallas kernels: 0 us -> 78.9 us
  matrix products: 17.6 us -> 0 us
  between operations: 15.9 us -> 2.4 us
  blocking collectives: 13.1 us -> 0 us
    reduce_scatter x1 -> x0, waiting for transfers between devices: 142 us -> none  [local(): lax.psum_scatter(factor * jnp.einsum('tf,td->fd', activations, upstream,...]
    pallas_call x0 -> x1, Pallas kernels: none -> 78.9 us  [local(): pl.pallas_call(functools.partial(kernel, bound), out_shape=(jax.ShapeDtyp...]
    all_gather x1 -> x0, waiting for transfers between devices: 42 us -> none  [local(): upstream = lax.all_gather(out_grad, 'tensor', axis=0, tiled=True)]
    dot_general x3 -> x0, matrix products: 17.6 us -> none  [the longest x1 11.7 us: local(): jnp.einsum('tf,td->fd', activations, upstream, preferred_element_type=jnp...]
    psum x1 -> x0, blocking collectives: 13.1 us -> none  [clip_factor(): sq_norm = lax.psum(partial_value, 'tensor')]
  transfers between devices with their start and end apart: 2 -> 0, of which waited for: 2 -> 0; matrix products, arithmetic and copies ran while one was open for 1% -> 0% of each run, Pallas kernels for 0% -> 0%
where the time goes in v1:
time: 83.4 us; the launch traced here: 83.3 us
  Pallas kernels  78.9 us (95%)
  between operations  2.4 us (3%)
  local copies, waits for them, and re-layouts  1.97 us (2%)
    pallas_call x1, Pallas kernels, local(): pl.pallas_call(functools.partial(kernel, bound), out_shape=(jax.ShapeDtyp...  78.9 us
    unnamed x1, local copies, waits for them, and re-layouts  1.97 us

profile of v1, /device:TPU:1, one launch (start us, length us, event | category | flops | bytes accessed | tf_op | source)
XLA Modules:
  0.0 83.3 jit_solution(7790218966396363277)
XLA Ops:
  0.6 78.9 %shard_map.59 = (f32[72,2304]{1,0:T(8,128)}, f32[1]{0:T(128)}) custom-call(bf16[512,2304]{1,0:T(8,128)(2,1)} %h_hbm.1, bf16[64,2304]{1,0:T(8,128)(2,1)} %g_hbm.1, f32[72,2304]{1,0:T(8,128)} %acc_hbm.1, f32[72,2304]{1,0:T(8,128)} %noise_hbm.1), custom_call_target="tpu_custom_call" | custom-call | tf_op jit(solution)/shard_map/pallas_call | solution.py:376
  79.5 2.0 %copy.8 = f32[72,2304]{1,0:T(8,128)} copy(f32[72,2304]{1,0:T(8,128)} %get-tuple-element.4) | data formatting | bytes 1327104

commit v2 on v1

--- a/solution.py
+++ b/solution.py
@@ -57,8 +57,10 @@
 
 def kernel(
     bound, h_hbm, g_hbm, acc_hbm, noise_hbm, out_ref, clip_ref,
-    hs, hp, ht, gs, gp, t, gram, norm, norms, send0, send1, recv0, recv1, sum0, sum1, fin, swap, acc, noise,
-    load_sem, gs_send, gs_recv, hp_send, hp_recv, gp_send, gp_recv, n_send, n_recv, rs_send, rs_recv, swap_sem,
+    hs, hp, ht, gs, gp, t, gram, norm, norms, send0, send1, recv0, recv1, last0, last1, sum0, sum1,
+    swap0, swap1, fin, acc, noise,
+    load_sem, gs_send, gs_recv, hp_send, hp_recv, gp_send, gp_recv, n_send, n_recv, rs_send, rs_recv, last_send, last_recv,
+    swap_send, swap_recv,
 ):
     dp, z = lax.axis_index("dp"), lax.axis_index("tensor")
     x, y, c = dp // 8, (dp // 2) % 4, dp % 2
@@ -66,6 +68,7 @@
     partner = (dp - c + o, z)
     along_z = ((dp, (z + 1) % 8), (dp, (z + 7) % 8))
     sends, recvs, sums = (send0, send1), (recv0, recv1), (sum0, sum1)
+    lasts, swaps = (last0, last1), (swap0, swap1)
 
     ia = (x * o + y * c, y * o + x * c)
     ib = (ia[1], ia[0])
@@ -91,9 +94,9 @@
     acc_load.start()
     noise_load.start()
 
-    others = [(dp, (z + k) % 8) for k in range(1, 8)]
-    others += [(partner[0], (z + k) % 8) for k in range(8)]
-    others += [device_of(0, 1, 0), device_of(0, -1, 0), device_of(0, 0, 1), device_of(0, 0, -1)]
+    others = [*along_z, partner]
+    for a, b in ((1, 0), (-1, 0), (0, 1), (0, -1)):
+        others += [device_of(0, a, b), (chunk_of(0, a, b) * 2 + o, z)]
     barrier = pltpu.get_barrier_semaphore()
     for device in others:
         pl.semaphore_signal(barrier, inc=1, device_id=device, device_id_type=MESH)
@@ -154,15 +157,11 @@
         total = fold(prod[:, lo:hi])
         return total if lo == 0 else total + 2.0 * fold(prod[:, 0:lo])
 
-    def terms(e, lo, first):
+    def terms(e):
         def body(i, _):
             r = pl.ds(pl.multiple_of(i * 256, 256), 256)
-            rhs = gs[lo : lo + 256, mine] if e == 0 else gp[lo : lo + 256, :]
-            value = jnp.dot(ht[e, r, lo : lo + 256], rhs, preferred_element_type=jnp.float32)
-            if first:
-                t[e, r, :] = value
-            else:
-                t[e, r, :] += value
+            rhs = gs[0:256, mine] if e == 0 else gp[0:256, :]
+            t[e, r, :] = jnp.dot(ht[e, r, 0:256], rhs, preferred_element_type=jnp.float32)
             return 0
 
         lax.fori_loop(0, FF // 256, body, 0)
@@ -185,11 +184,11 @@
             transpose(hp, 1)
         elif n == 8:
             norm[...] = out_gram(0, 256)
-            terms(0, 0, True)
+            terms(0)
         elif n == 9:
             for s in range(4):
                 give_g(s).wait_recv()
-            terms(1, 0, True)
+            terms(1)
         elif n == 11:
             norm[...] += out_gram(256, 384)
     give_g(7).start()
@@ -206,10 +205,22 @@
     pairs = [(e, k) for k in (4, 3, 5, 2, 6, 1, 7, 0) for e in range(2) if (e, k) != (0, 0)]
     for e, k in pairs:
         give_norm(e, k).start()
-    terms(0, 256, False)
     for s in range(4, 8):
         give_g(s).wait_recv()
-    terms(1, 256, False)
+
+    def finish(part, a, b):
+        rows = pl.ds(pl.multiple_of(chunk_of(part, a, b) * CHUNK, 16), CHUNK)
+        cols = slice(START[part], START[part] + WIDTH[part])
+        for e in range(2):
+            if e == 0:
+                rhs = gs[256:512, pl.ds(pl.multiple_of(c * HALF + START[part], 128), WIDTH[part])]
+            else:
+                rhs = gp[256:512, cols]
+            t[e, rows, cols] += jnp.dot(ht[e, rows, 256:512], rhs, preferred_element_type=jnp.float32)
+
+    for part in range(2):
+        for way in range(2):
+            finish(part, 2, ORDER[way][0])
     for e, k in pairs:
         give_norm(e, k).wait_recv()
 
@@ -224,7 +235,7 @@
     clip_ref[0] = f0
 
     limit = 2.0 * bound
-    scale = [REACH / (limit * chips) for chips in (1, 1, 2, 2, 2, 2, 4, 8)]
+    scale = [REACH / (limit * chips) for chips in (1, 1, 1, 1, 2, 2, 4, 8)]
 
     def own(part, chunk, r):
         rows = pl.ds(pl.multiple_of(chunk * CHUNK + r, 16), STEP)
@@ -252,13 +263,14 @@
         )
 
     def first_phase(part, way, slot):
-        sign = 1 - 2 * way
-        chunk = chunk_of(part, 2 if slot < 2 else sign, ORDER[way][slot])
+        a, b = 2 if slot < 2 else 1 - 2 * way, ORDER[way][slot]
+        if slot > 0:
+            finish(part, a, b)
         if slot >= 4:
             message(part, way, slot - 4).wait_recv()
 
         def body(r, rows):
-            value = own(part, chunk, r)
+            value = own(part, chunk_of(part, a, b), r)
             if slot >= 4:
                 value += decode(recvs[part][way, slot - 4, rows, :], 1.0 / scale[slot - 4])
             sends[part][way, slot, rows, :] = encode(value, scale[slot])
@@ -266,94 +278,38 @@
         over_rows(body)
         message(part, way, slot).start()
 
+    def own_sum(part, b):
+        finish(part, 0, b)
+
+        def body(r, rows):
+            sums[part][b, rows, :] = own(part, chunk_of(part, 0, b), r)
+
+        over_rows(body)
+
     def take(part, way, slot):
-        b = ORDER[way][slot]
         message(part, way, slot).wait_recv()
 
         def body(r, rows):
-            sums[part][b, rows, :] += decode(recvs[part][way, slot, rows, :], 1.0 / scale[slot])
+            sums[part][ORDER[way][slot], rows, :] += decode(recvs[part][way, slot, rows, :], 1.0 / scale[slot])
 
         over_rows(body)
 
-    for slot in range(4):
+    def both(step, slots):
         for way in range(2):
             for part in range(2):
-                first_phase(part, way, slot)
-    for part in range(2):
-        for b in range(4):
-            chunk = chunk_of(part, 0, b)
-
-            def body(r, rows):
-                sums[part][b, rows, :] = own(part, chunk, r)
-
-            over_rows(body)
-    for slot in (4, 5):
-        for way in range(2):
-            for part in range(2):
-                first_phase(part, way, slot)
-    for slot in (2, 3, 4):
-        for way in range(2):
-            for part in range(2):
-                take(part, way, slot)
-
-    for part in range(2):
-
-        def body(r, rows):
-            value = encode(sums[part][2, rows, :], scale[6])
-            for way in range(2):
-                sends[part][way, 6, rows, :] = value
-
-        over_rows(body)
-        for way in range(2):
-            message(part, way, 6).start()
-
-    def pass_on(part, way):
-        b = 1 if way == 0 else 3
-        rows = slice(0, TOP) if way == 0 else slice(TOP, CHUNK)
-        message(part, way, 6).wait_recv()
-        sums[part][b, rows, :] += decode(recvs[part][way, 6, rows, :], 1.0 / scale[6])
-
-        def body(r, rows):
-            sends[part][way, 7, rows, :] = encode(sums[part][b, rows, :], scale[7])
-
-        over_rows(body)
-        message(part, way, 7).start()
-
-    for part in range(2):
-        pass_on(part, 0)
-    for way in range(2):
+                step(part, way, slots[way])
+
+    both(first_phase, (0, 0))
+    both(first_phase, (2, 2))
+    for b in (2, 1):
         for part in range(2):
-            take(part, way, 5)
-    for part in range(2):
-        pass_on(part, 1)
-    for part in range(2):
-        for way in range(2):
-            message(part, way, 7).wait_recv()
-        cols = slice(START[part], START[part] + WIDTH[part])
-
-        def body(r, rows):
-            fin[rows, cols] = (
-                sums[part][0, rows, :]
-                + decode(recvs[part][0, 7, rows, :], 1.0 / scale[7])
-                + decode(recvs[part][1, 7, rows, :], 1.0 / scale[7])
-            )
-
-        over_rows(body)
-
-    my_rows = pl.ds(pl.multiple_of(c * (CHUNK // 2), 8), CHUNK // 2)
-    their_rows = pl.ds(pl.multiple_of(o * (CHUNK // 2), 8), CHUNK // 2)
-    exchange = pltpu.make_async_remote_copy(
-        src_ref=fin.at[their_rows], dst_ref=swap, send_sem=swap_sem.at[0], recv_sem=swap_sem.at[1],
-        device_id=partner, device_id_type=MESH,
-    )
-    exchange.start()
-    acc_load.wait()
-    noise_load.wait()
-    out_ref[:, mine] = acc[:, mine] + fin[my_rows, :] + noise[:, mine]
-    exchange.wait_recv()
-    out_ref[:, theirs] = acc[:, theirs] + swap[...] + noise[:, theirs]
-
-    exchange.wait_send()
+            own_sum(part, b)
+    both(first_phase, (4, 4))
+    both(first_phase, (1, 1))
+    for b in (3, 0):
+        for part in range(2):
+            own_sum(part, b)
+
     for way in range(2):
         for n in range(GATHER):
             gather(way, n).wait_send()
@@ -362,10 +318,90 @@
         give_g(s).wait_send()
     for e, k in pairs:
         give_norm(e, k).wait_send()
-    for part in range(2):
-        for way in range(2):
-            for slot in range(8):
+
+    both(take, (2, 2))
+    both(take, (4, 4))
+
+    for part in range(2):
+
+        def body(r, rows):
+            value = encode(sums[part][2, rows, :], scale[6])
+            for way in range(2):
+                sends[part][way, 6, rows, :] = value
+
+        over_rows(body)
+        for way in range(2):
+            message(part, way, 6).start()
+
+    both(first_phase, (5, 3))
+    both(first_phase, (3, 5))
+
+    def window(core):
+        return pl.ds(pl.multiple_of(core * (CHUNK - TOP), 16), TOP)
+
+    def last(part, way, which):
+        core = c if which == 0 else o
+        return pltpu.make_async_remote_copy(
+            src_ref=sends[part].at[way, 7, window(core)], dst_ref=lasts[part].at[which, way],
+            send_sem=last_send.at[part, way, which], recv_sem=last_recv.at[part, way, which],
+            device_id=(chunk_of(part, 0, 1 - 2 * way) * 2 + core, z), device_id_type=MESH,
+        )
+
+    def pass_on(part, way):
+        b = 1 if way == 0 else 3
+        rows = slice(0, TOP) if way == 0 else slice(TOP, CHUNK)
+        message(part, way, 6).wait_recv()
+        sums[part][b, rows, :] += decode(recvs[part][way, 6, rows, :], 1.0 / scale[6])
+
+        def body(r, rows):
+            sends[part][way, 7, rows, :] = encode(sums[part][b, rows, :], scale[7])
+
+        over_rows(body)
+        for which in range(2):
+            last(part, way, which).start()
+
+    for part in range(2):
+        pass_on(part, 0)
+    both(take, (5, 3))
+    for part in range(2):
+        pass_on(part, 1)
+    both(take, (3, 5))
+
+    def swap(part):
+        return pltpu.make_async_remote_copy(
+            src_ref=sums[part].at[0, window(o)], dst_ref=swaps[part],
+            send_sem=swap_send.at[part], recv_sem=swap_recv.at[part], device_id=partner, device_id_type=MESH,
+        )
+
+    for part in range(2):
+        swap(part).start()
+    acc_load.wait()
+    noise_load.wait()
+    out_ref[...] = acc[...] + noise[...]
+    for part in range(2):
+        swap(part).wait_recv()
+        for way in range(2):
+            for slot in range(7):
                 message(part, way, slot).wait_send()
+
+    for part in range(2):
+        cols = slice(START[part], START[part] + WIDTH[part])
+        for which in range(2):
+            for way in range(2):
+                last(part, way, which).wait_recv()
+            value = sums[part][0, window(c), :] if which == 0 else swaps[part][...]
+            for way in range(2):
+                value += decode(lasts[part][which, way], 1.0 / scale[7])
+            fin[which, :, cols] = value
+    kept = pl.ds(pl.multiple_of(c * 8, 8), CHUNK // 2)
+    out_ref[:, mine] += fin[0, kept, :]
+    out_ref[:, theirs] += fin[1, kept, :]
+
+    for part in range(2):
+        swap(part).wait_send()
+        for way in range(2):
+            for which in range(2):
+                last(part, way, which).wait_send()
 
 
 def local(activations, out_grad, accum, noise):
@@ -392,10 +428,13 @@
             pltpu.VMEM((2, 8, CHUNK, WIDTH[1]), bf16),
             pltpu.VMEM((2, 8, CHUNK, WIDTH[0]), bf16),
             pltpu.VMEM((2, 8, CHUNK, WIDTH[1]), bf16),
+            pltpu.VMEM((2, 2, TOP, WIDTH[0]), bf16),
+            pltpu.VMEM((2, 2, TOP, WIDTH[1]), bf16),
             pltpu.VMEM((4, CHUNK, WIDTH[0]), f32),
             pltpu.VMEM((4, CHUNK, WIDTH[1]), f32),
-            pltpu.VMEM((CHUNK, HALF), f32),
-            pltpu.VMEM((CHUNK // 2, HALF), f32),
+            pltpu.VMEM((TOP, WIDTH[0]), f32),
+            pltpu.VMEM((TOP, WIDTH[1]), f32),
+            pltpu.VMEM((2, TOP, HALF), f32),
             pltpu.VMEM(accum.shape, f32),
             pltpu.VMEM(accum.shape, f32),
             dma((11,)),
@@ -409,6 +448,9 @@
             dma((2, 8)),
             dma((2, 2, 8)),
             dma((2, 2, 8)),
+            dma((2, 2, 2)),
+            dma((2, 2, 2)),
+            dma((2,)),
             dma((2,)),
         ],
         compiler_params=pltpu.CompilerParams(

time: 83.4 us -> 79.5 us (0.953)
  Pallas kernels: 78.9 us -> 74.9 us
    pallas_call x1, Pallas kernels: 78.9 us -> 74.9 us  [local(): pl.pallas_call(functools.partial(kernel, bound), out_shape=(jax.ShapeDtyp...]
where the time goes in v2:
time: 79.5 us; the launch traced here: 79.3 us
  Pallas kernels  74.9 us (94%)
  between operations  2.4 us (3%)
  local copies, waits for them, and re-layouts  1.97 us (2%)
    pallas_call x1, Pallas kernels, local(): pl.pallas_call(functools.partial(kernel, bound), out_shape=(jax.ShapeDtyp...  74.9 us
    unnamed x1, local copies, waits for them, and re-layouts  1.97 us

profile of v2, /device:TPU:1, one launch (start us, length us, event | category | flops | bytes accessed | tf_op | source)
XLA Modules:
  0.0 79.3 jit_solution(6704466385431884548)
XLA Ops:
  0.6 74.9 %shard_map.59 = (f32[72,2304]{1,0:T(8,128)}, f32[1]{0:T(128)}) custom-call(bf16[512,2304]{1,0:T(8,128)(2,1)} %h_hbm.1, bf16[64,2304]{1,0:T(8,128)(2,1)} %g_hbm.1, f32[72,2304]{1,0:T(8,128)} %acc_hbm.1, f32[72,2304]{1,0:T(8,128)} %noise_hbm.1), custom_call_target="tpu_custom_call" | custom-call | tf_op jit(solution)/shard_map/pallas_call | solution.py:412
  75.6 2.0 %copy.8 = f32[72,2304]{1,0:T(8,128)} copy(f32[72,2304]{1,0:T(8,128)} %get-tuple-element.4) | data formatting | bytes 1327104

commit v3 on v2

v3 whole, which is shorter than its diff:
```python
import functools
import math

import jax
import jax.numpy as jnp
from jax import lax
from jax.experimental import pallas as pl
from jax.experimental.pallas import tpu as pltpu
from jax.sharding import PartitionSpec as P

MESH = pl.DeviceIdType.MESH
LEN = 512
FF = 2304
D = 2304
HALF = D // 2
ROWS = 64
SUB = 16
NSUB = ROWS // SUB
CHUNK = 144
WIDTH = (640, 512)
START = (0, 640)
STEP = 48
TOP = 80

PHASE_START = (0, 512, 896)
PHASE_WIDTH = (512, 384, 256)
PIECE_WIDTH = ((256, 256, 128), (256, 128, 128))
PIECE_START = ((0, 256, 512), (0, 256, 384))

SLOT = ((0, 1, 3, 5, 7), (0, 2, 4, 6, 7))
SUBS = ((0, 1, 2, 3), (2, 3, 0, 1))
BLOCK = (0, -1, 1, -2, 2, -3, 3, 4)
GATHER = 14
SEQUENCE = (
    (0, 1), (2, 3), (0, 0), (0, 2), (0, 3), (1, 0), (2, 0), (0, 5), (2, 1), (1, 3), (0, 4),
    (1, 2), (0, 7), (1, 1), (0, 9), (0, 6), (0, 8), (1, 4), (0, 11), (1, 5), (0, 13), (0, 10),
    (2, 2), (0, 12), (2, 4), (2, 5), (1, 6), (1, 8), (1, 9), (1, 7), (2, 7), (2, 6), (2, 8),
    (2, 9), (1, 10), (1, 12), (1, 13), (1, 11), (2, 11), (2, 10), (2, 12), (2, 13),
)
SPARE = (0.6, 0.45, 0.3)
GROUPS = ((0, 64), (64, 192), (192, 320), (320, 448), (448, 512))

ORDER = ((1, 0, 2, 3), (2, 3, 1, 0))
AHEAD = ((2, 3), (1, 0))

POWER = 9
REACH = 2.0**14
AHEAD_SCALE = 0.9


def encode(x, scale):
    y = x * scale
    y2 = y * y
    y4 = y2 * y2
    return (y4 * y4 * y).astype(jnp.bfloat16)


def decode(sent, unscale):
    z = sent.astype(jnp.float32)
    r = jnp.exp(jnp.log(jnp.abs(z)) * (1.0 / POWER)) * unscale
    return jnp.where(z < 0, -r, r)


def fold(prod):
    total = None
    for i in range(0, prod.shape[0], 8):
        for j in range(0, prod.shape[1], 128):
            piece = prod[i : i + 8, j : j + 128]
            total = piece if total is None else total + piece
    return total


def kernel(
    bound, h_hbm, g_hbm, acc_hbm, noise_hbm, out_ref, clip_ref,
    hs, hp, ht, gs0, gs1, gs2, gp0, gp1, gp2, t, gram, norm, norms, factors, others_factors,
    as00, as01, as02, as10, as11, as12, ar00, ar01, ar02, ar10, ar11, ar12,
    send0, send1, recv0, recv1, last0, last1, sum0, sum1, swap0, swap1, fin, acc, noise,
    load_sem, gs_send, gs_recv, hp_send, hp_recv, gp_send, gp_recv, n_send, n_recv, f_send, f_recv, a_send, a_recv,
    rs_send, rs_recv, last_send, last_recv, swap_send, swap_recv,
):
    gs, gp = (gs0, gs1, gs2), (gp0, gp1, gp2)
    asend, arecv = ((as00, as01, as02), (as10, as11, as12)), ((ar00, ar01, ar02), (ar10, ar11, ar12))
    dp, z = lax.axis_index("dp"), lax.axis_index("tensor")
    x, y, c = dp // 8, (dp // 2) % 4, dp % 2
    o = 1 - c
    partner = (dp - c + o, z)
    along_z = ((dp, (z + 1) % 8), (dp, (z + 7) % 8))
    sends, recvs, sums = (send0, send1), (recv0, recv1), (sum0, sum1)
    lasts, swaps = (last0, last1), (swap0, swap1)

    ia = (x * o + y * c, y * o + x * c)
    ib = (ia[1], ia[0])
    step_a = (4 * o + c, o + 4 * c)
    step_b = (step_a[1], step_a[0])

    def chunk_of(part, a, b):
        return ((ia[part] + a + 4) % 4) * step_a[part] + ((ib[part] + b + 4) % 4) * step_b[part]

    def device_of(part, a, b):
        return (chunk_of(part, a, b) * 2 + c, z)

    loads = []
    for s in range(8):
        row = pl.multiple_of(((z + BLOCK[s] + 8) % 8) * ROWS, ROWS)
        loads.append(pltpu.make_async_copy(h_hbm.at[pl.ds(row, ROWS)], hs.at[pl.ds(s * ROWS, ROWS)], load_sem.at[s]))
    g_loads = []
    for j in range(3):
        for half in range(2):
            src = g_hbm.at[:, pl.ds(half * HALF + PHASE_START[j], PHASE_WIDTH[j])]
            dst = gs[j].at[pl.ds(0, ROWS), pl.ds(half * PHASE_WIDTH[j], PHASE_WIDTH[j])]
            g_loads.append(pltpu.make_async_copy(src, dst, load_sem.at[8 + 2 * j + half]))
    acc_load = pltpu.make_async_copy(acc_hbm, acc, load_sem.at[14])
    noise_load = pltpu.make_async_copy(noise_hbm, noise, load_sem.at[15])
    for copy in g_loads:
        copy.start()
    for copy in loads:
        copy.start()
    acc_load.start()
    noise_load.start()

    others = [*along_z, partner]
    for a, b in ((1, 0), (-1, 0), (0, 1), (0, -1)):
        others += [device_of(0, a, b), (chunk_of(0, a, b) * 2 + o, z)]
    barrier = pltpu.get_barrier_semaphore()
    for device in others:
        pl.semaphore_signal(barrier, inc=1, device_id=device, device_id_type=MESH)
    pl.semaphore_wait(barrier, len(others))

    def gather(j, way, n):
        sub = SUBS[way][n % NSUB]
        src = gs[j].at[pl.ds(SLOT[way][n // NSUB] * ROWS + sub * SUB, SUB)]
        dst = gs[j].at[pl.ds(SLOT[way][n // NSUB + 1] * ROWS + sub * SUB, SUB)]
        return pltpu.make_async_remote_copy(
            src_ref=src, dst_ref=dst, send_sem=gs_send.at[j, way, n], recv_sem=gs_recv.at[j, way, n],
            device_id=along_z[way], device_id_type=MESH,
        )

    def give_h(s):
        return pltpu.make_async_remote_copy(
            src_ref=hs.at[pl.ds(s * ROWS, ROWS)], dst_ref=hp.at[pl.ds(s * ROWS, ROWS)],
            send_sem=hp_send.at[s], recv_sem=hp_recv.at[s], device_id=partner, device_id_type=MESH,
        )

    def give_g(j, group):
        lo, hi = GROUPS[group]
        cols = pl.ds(pl.multiple_of(o * PHASE_WIDTH[j], 128), PHASE_WIDTH[j])
        return pltpu.make_async_remote_copy(
            src_ref=gs[j].at[pl.ds(lo, hi - lo), cols], dst_ref=gp[j].at[pl.ds(lo, hi - lo)],
            send_sem=gp_send.at[j, group], recv_sem=gp_recv.at[j, group], device_id=partner, device_id_type=MESH,
        )

    def act_gram(i, _):
        r = pl.ds(pl.multiple_of(i * 128, 128), 128)
        gram[r, :] = lax.dot_general(
            hs[r, :], hs[...], (((1,), (1,)), ((), ())), preferred_element_type=jnp.float32
        )
        return 0

    def transpose(src, e, lo, hi):
        def body(i, _):
            r = pl.ds(pl.multiple_of(i * 128, 128), 128)
            ht[e, r, :] = src[:, r].T
            return 0

        lax.fori_loop(lo, hi, body, 0)

    def out_gram(j, lo, hi):
        prod = gram[lo:hi, 0:hi] * lax.dot_general(
            gs[j][lo:hi, :], gs[j][0:hi, :], (((1,), (1,)), ((), ())), preferred_element_type=jnp.float32
        )
        total = fold(prod[:, lo:hi])
        if lo > 0:
            total += 2.0 * fold(prod[:, 0:lo])
        if j == 0 and lo == 0:
            norm[...] = total
        else:
            norm[...] += total

    def term(e, part, j, chunk):
        rows = pl.ds(pl.multiple_of(chunk * CHUNK, 16), CHUNK)
        skip = 0 if part == 0 else PIECE_WIDTH[0][j]
        if e == 0:
            cols = pl.ds(pl.multiple_of(c * PHASE_WIDTH[j] + skip, 128), PIECE_WIDTH[part][j])
            rhs = gs[j][:, cols]
        else:
            rhs = gp[j][:, skip : skip + PIECE_WIDTH[part][j]]
        return jnp.dot(ht[e, rows, :], rhs, preferred_element_type=jnp.float32)

    def prepare(part, a, b, phases):
        chunk = chunk_of(part, a, b)
        rows = pl.ds(pl.multiple_of(chunk * CHUNK, 16), CHUNK)
        for j in phases:
            start = START[part] + PIECE_START[part][j]
            for e in range(2):
                t[e, rows, start : start + PIECE_WIDTH[part][j]] = term(e, part, j, chunk)

    def ahead(part, way, j):
        return pltpu.make_async_remote_copy(
            src_ref=asend[part][j].at[way], dst_ref=arecv[part][j].at[way],
            send_sem=a_send.at[part, way, j], recv_sem=a_recv.at[part, way, j],
            device_id=device_of(part, 1 - 2 * way, 0), device_id_type=MESH,
        )

    def send_ahead(part, way, j):
        for k in range(2):
            for e in range(2):
                value = term(e, part, j, chunk_of(part, 2, AHEAD[way][k]))
                asend[part][j][way, k, e] = encode(value, AHEAD_SCALE)
        ahead(part, way, j).start()

    for copy in g_loads:
        copy.wait()
    received, sent = set(), 0

    def forward(sent):
        while sent < len(SEQUENCE):
            j, n = SEQUENCE[sent]
            if n >= NSUB and (j, n - NSUB) not in received:
                break
            for way in range(2):
                gather(j, way, n).start()
            sent += 1
        return sent

    sent = forward(sent)
    for j in range(3):
        give_g(j, 0).start()
    for s in range(8):
        loads[s].wait()
        give_h(s).start()

    def wait_h():
        for s in range(8):
            give_h(s).wait_recv()

    def wait_g(j):
        for group in range(5):
            give_g(j, group).wait_recv()

    first = [(part, way) for way in range(2) for part in range(2)]

    work = [(None, 0.3, functools.partial(lax.fori_loop, i, i + 1, act_gram, 0)) for i in range(4)]
    work += [(None, 0.4, functools.partial(transpose, hs, 0, i, i + 3)) for i in range(0, 18, 3)]
    work += [(None, 0.1, functools.partial(wait_h))]
    work += [(None, 0.4, functools.partial(transpose, hp, 1, i, i + 3)) for i in range(0, 18, 3)]
    later = []
    for j in range(3):
        here = (j, GATHER)
        terms_of = [(here, 0.1, functools.partial(wait_g, j))]
        terms_of += [(here, 0.5 - 0.1 * j, functools.partial(send_ahead, part, way, j)) for part, way in first]
        work += [
            ((j, need), 0.2, functools.partial(out_gram, j, lo, hi))
            for need, lo, hi in ((8, 0, 256), (12, 256, 384), (14, 384, 512))
        ]
        ready = [
            (here, 0.2, functools.partial(prepare, part, 1 - 2 * way, ORDER[way][0], (j,))) for part, way in first
        ]
        if j < 2:
            work += terms_of
            later += ready
        else:
            work += later
            late = terms_of[:1] + ready
            late += [
                (here, 0.2, functools.partial(prepare, part, 2, b, (j,))) for part, way in first for b in AHEAD[way]
            ]

    spare, steps, whole, taken = 0.0, 0, {}, set()
    for j, n in SEQUENCE:
        for way in range(2):
            gather(j, way, n).wait_recv()
        received.add((j, n))
        sent = forward(sent)
        d = n // NSUB
        if {(j, k) for k in range(d * NSUB, min(d * NSUB + NSUB, GATHER))} <= received:
            give_g(j, d + 1).start()
        spare = SPARE[j] + min(spare, 0.3)
        steps += 1
        for phase in range(3):
            if phase not in whole and {(phase, k) for k in range(GATHER)} <= received:
                whole[phase] = steps
        for entry in list(work):
            gate, cost, item = entry
            if item.func is wait_g:
                ready = steps >= whole.get(gate[0], steps) + 2
            else:
                ready = gate is None or {(gate[0], k) for k in range(gate[1])} <= received
                ready = ready and not (item.func in (send_ahead, prepare) and gate[0] not in taken)
            if ready and spare >= cost:
                item()
                spare -= cost
                work.remove(entry)
                if item.func is wait_g:
                    taken.add(gate[0])

    late = [entry for entry in work if entry[2].func is not out_gram] + late
    for _, _, item in work:
        if item.func is out_gram:
            item()

    def give_norm(e, k):
        device = (dp if e == 0 else partner[0], (z + k) % 8)
        return pltpu.make_async_remote_copy(
            src_ref=norm, dst_ref=norms.at[e, k], send_sem=n_send.at[e, k], recv_sem=n_recv.at[e, k],
            device_id=device, device_id_type=MESH,
        )

    pairs = [(e, k) for k in (4, 3, 5, 2, 6, 1, 7, 0) for e in range(2) if (e, k) != (0, 0)]
    for e, k in pairs:
        give_norm(e, k).start()
    for _, _, item in late:
        item()
    for e, k in pairs:
        give_norm(e, k).wait_recv()

    def factor(e):
        total = norm[...] if e == 0 else norms[1, 0]
        for k in range(1, 8):
            total = total + norms[e, k]
        sq_norm = jnp.broadcast_to(jnp.sum(total), (8, 128))
        factors[e] = jnp.minimum(1.0, bound / jnp.sqrt(sq_norm))
        return jnp.max(factors[e])

    f0, f1 = factor(0), factor(1)
    clip_ref[0] = f0

    def give_factors(part, way):
        return pltpu.make_async_remote_copy(
            src_ref=factors, dst_ref=others_factors.at[part, way], send_sem=f_send.at[part, way],
            recv_sem=f_recv.at[part, way], device_id=device_of(part, 1 - 2 * way, 0), device_id_type=MESH,
        )


    limit = 2.0 * bound
    scale = [REACH / (limit * chips) for chips in (1, 1, 2, 2, 4, 8)]

    def own(part, chunk, r):
        rows = pl.ds(pl.multiple_of(chunk * CHUNK + r, 16), STEP)
        cols = slice(START[part], START[part] + WIDTH[part])
        return f0 * t[0, rows, cols] + f1 * t[1, rows, cols]

    def over_rows(body):
        def step(i, _):
            r = pl.multiple_of(i * STEP, 16)
            body(r, pl.ds(r, STEP))
            return 0

        lax.fori_loop(0, CHUNK // STEP, step, 0)

    def send_last_phase(part, way):
        cols = slice(START[part] + PIECE_START[part][2], START[part] + WIDTH[part])
        for k in range(2):
            chunk = chunk_of(part, 2, AHEAD[way][k])

            def body(r, rows):
                mine = pl.ds(pl.multiple_of(chunk * CHUNK + r, 16), STEP)
                value = f0 * t[0, mine, cols] + f1 * t[1, mine, cols]
                asend[part][2][way, k, 0, rows, :] = encode(value, scale[0])

            over_rows(body)
        ahead(part, way, 2).start()

    for part in range(2):
        for way in range(2):
            give_factors(part, way).start()
            send_last_phase(part, way)

    def message(part, way, slot):
        sign = 1 - 2 * way
        rows = pl.ds(0, CHUNK)
        if slot == 4:
            rows = pl.ds(0, TOP) if way == 0 else pl.ds(TOP, CHUNK - TOP)
        device = device_of(part, sign, 0) if slot < 4 else device_of(part, 0, sign)
        return pltpu.make_async_remote_copy(
            src_ref=sends[part].at[way, slot, rows], dst_ref=recvs[part].at[way, slot, rows],
            send_sem=rs_send.at[part, way, slot], recv_sem=rs_recv.at[part, way, slot],
            device_id=device, device_id_type=MESH,
        )

    def first_phase(part, way, slot):
        a, b = 1 - 2 * way, ORDER[way][slot]
        if slot > 0:
            prepare(part, a, b, (0, 1, 2))
        if slot == 2:
            give_factors(part, way).wait_recv()
            for j in range(3):
                ahead(part, way, j).wait_recv()
        if slot >= 2:
            their_f = [jnp.max(others_factors[part, way, e]) for e in range(2)]

        def body(r, rows):
            value = own(part, chunk_of(part, a, b), r)
            if slot < 2:
                sends[part][way, slot, rows, :] = encode(value, scale[slot])
                return
            for j in range(3):
                start = PIECE_START[part][j]
                piece = value[:, start : start + PIECE_WIDTH[part][j]]
                if j == 2:
                    piece += decode(arecv[part][j][way, slot - 2, 0, rows, :], 1.0 / scale[0])
                else:
                    for e in range(2):
                        piece += their_f[e] * decode(arecv[part][j][way, slot - 2, e, rows, :], 1.0 / AHEAD_SCALE)
                sends[part][way, slot, rows, start : start + PIECE_WIDTH[part][j]] = encode(piece, scale[slot])

        over_rows(body)
        message(part, way, slot).start()

    def own_sum(part, b):
        prepare(part, 0, b, (0, 1, 2))

        def body(r, rows):
            sums[part][b, rows, :] = own(part, chunk_of(part, 0, b), r)

        over_rows(body)

    def take(part, way, slot):
        message(part, way, slot).wait_recv()

        def body(r, rows):
            sums[part][ORDER[way][slot], rows, :] += decode(recvs[part][way, slot, rows, :], 1.0 / scale[slot])

        over_rows(body)

    def both(step, slots):
        for way in range(2):
            for part in range(2):
                step(part, way, slots[way])

    both(first_phase, (0, 0))
    for b in (2, 1):
        for part in range(2):
            own_sum(part, b)
    both(first_phase, (2, 2))
    both(first_phase, (3, 1))
    for b in (3, 0):
        for part in range(2):
            own_sum(part, b)

    for j in range(3):
        for way in range(2):
            for n in range(GATHER):
                gather(j, way, n).wait_send()
            for part in range(2):
                ahead(part, way, j).wait_send()
        for group in range(5):
            give_g(j, group).wait_send()
    for s in range(8):
        give_h(s).wait_send()
    for e, k in pairs:
        give_norm(e, k).wait_send()
    for part in range(2):
        for way in range(2):
            give_factors(part, way).wait_send()

    both(take, (0, 0))
    both(take, (2, 2))

    for part in range(2):

        def body(r, rows):
            value = encode(sums[part][2, rows, :], scale[4])
            for way in range(2):
                sends[part][way, 4, rows, :] = value

        over_rows(body)
        for way in range(2):
            message(part, way, 4).start()

    both(first_phase, (1, 3))

    def window(core):
        return pl.ds(pl.multiple_of(core * (CHUNK - TOP), 16), TOP)

    def last(part, way, which):
        core = c if which == 0 else o
        return pltpu.make_async_remote_copy(
            src_ref=sends[part].at[way, 5, window(core)], dst_ref=lasts[part].at[which, way],
            send_sem=last_send.at[part, way, which], recv_sem=last_recv.at[part, way, which],
            device_id=(chunk_of(part, 0, 1 - 2 * way) * 2 + core, z), device_id_type=MESH,
        )

    def pass_on(part, way):
        b = 1 if way == 0 else 3
        rows = slice(0, TOP) if way == 0 else slice(TOP, CHUNK)
        message(part, way, 4).wait_recv()
        sums[part][b, rows, :] += decode(recvs[part][way, 4, rows, :], 1.0 / scale[4])

        def body(r, rows):
            sends[part][way, 5, rows, :] = encode(sums[part][b, rows, :], scale[5])

        over_rows(body)
        for which in range(2):
            last(part, way, which).start()

    for part in range(2):
        pass_on(part, 0)
    both(take, (3, 1))
    for part in range(2):
        pass_on(part, 1)
    both(take, (1, 3))

    def swap(part):
        return pltpu.make_async_remote_copy(
            src_ref=sums[part].at[0, window(o)], dst_ref=swaps[part],
            send_sem=swap_send.at[part], recv_sem=swap_recv.at[part], device_id=partner, device_id_type=MESH,
        )

    for part in range(2):
        swap(part).start()
    acc_load.wait()
    noise_load.wait()
    out_ref[...] = acc[...] + noise[...]
    for part in range(2):
        swap(part).wait_recv()
        for way in range(2):
            for slot in range(5):
                message(part, way, slot).wait_send()

    for part in range(2):
        cols = slice(START[part], START[part] + WIDTH[part])
        for which in range(2):
            for way in range(2):
                last(part, way, which).wait_recv()
            value = sums[part][0, window(c), :] if which == 0 else swaps[part][...]
            for way in range(2):
                value += decode(lasts[part][which, way], 1.0 / scale[5])
            fin[which, :, cols] = value
    kept = pl.ds(pl.multiple_of(c * 8, 8), CHUNK // 2)
    for which in range(2):
        for part in range(2):
            for j in range(3):
                width = PIECE_WIDTH[part][j]
                skip = PHASE_START[j] + (0 if part == 0 else PIECE_WIDTH[0][j])
                start = START[part] + PIECE_START[part][j]
                cols = pl.ds(pl.multiple_of((c if which == 0 else o) * HALF + skip, 128), width)
                out_ref[:, cols] += fin[which, kept, start : start + width]

    for part in range(2):
        swap(part).wait_send()
        for way in range(2):
            for which in range(2):
                last(part, way, which).wait_send()


def local(activations, out_grad, accum, noise):
    hidden_all = activations.shape[1] * lax.axis_size("tensor")
    bound = 0.02 * math.sqrt(activations.shape[0] * hidden_all * out_grad.shape[1])
    f32, bf16, dma = jnp.float32, jnp.bfloat16, pltpu.SemaphoreType.DMA
    hbm = pl.BlockSpec(memory_space=pl.ANY)
    return pl.pallas_call(
        functools.partial(kernel, bound),
        out_shape=(jax.ShapeDtypeStruct(accum.shape, f32), jax.ShapeDtypeStruct((1,), f32)),
        in_specs=[hbm] * 4,
        out_specs=(pl.BlockSpec(memory_space=pltpu.VMEM), pl.BlockSpec(memory_space=pltpu.SMEM)),
        scratch_shapes=[
            pltpu.VMEM((LEN, FF), bf16),
            pltpu.VMEM((LEN, FF), bf16),
            pltpu.VMEM((2, FF, LEN), bf16),
            *[pltpu.VMEM((LEN, 2 * width), bf16) for width in PHASE_WIDTH],
            *[pltpu.VMEM((LEN, width), bf16) for width in PHASE_WIDTH],
            pltpu.VMEM((2, FF, HALF), f32),
            pltpu.VMEM((LEN, LEN), f32),
            pltpu.VMEM((8, 128), f32),
            pltpu.VMEM((2, 8, 8, 128), f32),
            pltpu.VMEM((2, 8, 128), f32),
            pltpu.VMEM((2, 2, 2, 8, 128), f32),
            *[pltpu.VMEM((2, 2, 2 - j // 2, CHUNK, part[j]), bf16) for part in PIECE_WIDTH for j in range(3)] * 2,
            pltpu.VMEM((2, 6, CHUNK, WIDTH[0]), bf16),
            pltpu.VMEM((2, 6, CHUNK, WIDTH[1]), bf16),
            pltpu.VMEM((2, 6, CHUNK, WIDTH[0]), bf16),
            pltpu.VMEM((2, 6, CHUNK, WIDTH[1]), bf16),
            pltpu.VMEM((2, 2, TOP, WIDTH[0]), bf16),
            pltpu.VMEM((2, 2, TOP, WIDTH[1]), bf16),
            pltpu.VMEM((4, CHUNK, WIDTH[0]), f32),
            pltpu.VMEM((4, CHUNK, WIDTH[1]), f32),
            pltpu.VMEM((TOP, WIDTH[0]), f32),
            pltpu.VMEM((TOP, WIDTH[1]), f32),
            pltpu.VMEM((2, TOP, HALF), f32),
            pltpu.VMEM(accum.shape, f32),
            pltpu.VMEM(accum.shape, f32),
            dma((16,)),
            dma((3, 2, GATHER)),
            dma((3, 2, GATHER)),
            dma((8,)),
            dma((8,)),
            dma((3, 5)),
            dma((3, 5)),
            dma((2, 8)),
            dma((2, 8)),
            dma((2, 2)),
            dma((2, 2)),
            dma((2, 2, 3)),
            dma((2, 2, 3)),
            dma((2, 2, 5)),
            dma((2, 2, 5)),
            dma((2, 2, 2)),
            dma((2, 2, 2)),
            dma((2,)),
            dma((2,)),
        ],
        compiler_params=pltpu.CompilerParams(
            collective_id=0, has_side_effects=True, vmem_limit_bytes=62 * 2**20
        ),
    )(activations, out_grad, accum, noise)


def solution(mesh):
    in_specs = (
        P("dp", "tensor"),
        P(("dp", "tensor"), None),
        P(("tensor", "dp"), None),
        P(("tensor", "dp"), None),
    )
    out_specs = (P(("tensor", "dp"), None), P("dp"))
    return jax.shard_map(local, mesh=mesh, in_specs=in_specs, out_specs=out_specs, check_vma=False)
```

time: 79.5 us -> 76 us (0.956)
  Pallas kernels: 74.9 us -> 71.5 us
    pallas_call x1, Pallas kernels: 74.9 us -> 71.5 us  [local(): pl.pallas_call(functools.partial(kernel, bound), out_shape=(jax.ShapeDtyp...]
where the time goes in v3:
time: 76 us; the launch traced here: 75.8 us
  Pallas kernels  71.5 us (94%)
  between operations  2.4 us (3%)
  local copies, waits for them, and re-layouts  1.97 us (3%)
    pallas_call x1, Pallas kernels, local(): pl.pallas_call(functools.partial(kernel, bound), out_shape=(jax.ShapeDtyp...  71.5 us
    unnamed x1, local copies, waits for them, and re-layouts  1.97 us

profile of v3, /device:TPU:1, one launch (start us, length us, event | category | flops | bytes accessed | tf_op | source)
XLA Modules:
  0.0 75.8 jit_solution(2383163248344202279)
XLA Ops:
  0.6 71.5 %shard_map.59 = (f32[72,2304]{1,0:T(8,128)}, f32[1]{0:T(128)}) custom-call(bf16[512,2304]{1,0:T(8,128)(2,1)} %h_hbm.1, bf16[64,2304]{1,0:T(8,128)(2,1)} %g_hbm.1, f32[72,2304]{1,0:T(8,128)} %acc_hbm.1, f32[72,2304]{1,0:T(8,128)} %noise_hbm.1), custom_call_target="tpu_custom_call" | custom-call | tf_op jit(solution)/shard_map/pallas_call | solution.py:551
  72.1 2.0 %copy.8 = f32[72,2304]{1,0:T(8,128)} copy(f32[72,2304]{1,0:T(8,128)} %get-tuple-element.4) | data formatting | bytes 1327104

commit v4 on v3

--- a/solution.py
+++ b/solution.py
@@ -37,19 +37,21 @@
     (2, 2), (0, 12), (2, 4), (2, 5), (1, 6), (1, 8), (1, 9), (1, 7), (2, 7), (2, 6), (2, 8),
     (2, 9), (1, 10), (1, 12), (1, 13), (1, 11), (2, 11), (2, 10), (2, 12), (2, 13),
 )
-SPARE = (0.6, 0.45, 0.3)
+SPARE = (0.6, 0.45, 0.4)
 GROUPS = ((0, 64), (64, 192), (192, 320), (320, 448), (448, 512))
 
 ORDER = ((1, 0, 2, 3), (2, 3, 1, 0))
 AHEAD = ((2, 3), (1, 0))
 
 POWER = 9
-REACH = 2.0**14
-AHEAD_SCALE = 0.9
+REACH = 2.0**13.5
+LARGEST = 2.0**14.1
+TINY = 1e-30
+CHIP, TERM = 2, 3
 
 
 def encode(x, scale):
-    y = x * scale
+    y = jnp.clip(x * scale, -LARGEST, LARGEST)
     y2 = y * y
     y4 = y2 * y2
     return (y4 * y4 * y).astype(jnp.bfloat16)
@@ -62,20 +64,20 @@
 
 
 def fold(prod):
-    total = None
-    for i in range(0, prod.shape[0], 8):
-        for j in range(0, prod.shape[1], 128):
-            piece = prod[i : i + 8, j : j + 128]
-            total = piece if total is None else total + piece
-    return total
+    pieces = [
+        prod[i : i + 8, j : j + 128] for i in range(0, prod.shape[0], 8) for j in range(0, prod.shape[1], 128)
+    ]
+    while len(pieces) > 1:
+        pieces = [pieces[i] + pieces[i + 1] if i + 1 < len(pieces) else pieces[i] for i in range(0, len(pieces), 2)]
+    return pieces[0]
 
 
 def kernel(
     bound, h_hbm, g_hbm, acc_hbm, noise_hbm, out_ref, clip_ref,
-    hs, hp, ht, gs0, gs1, gs2, gp0, gp1, gp2, t, gram, norm, norms, factors, others_factors,
+    hs, hp, ht, gs0, gs1, gs2, gp0, gp1, gp2, t, gram, norm, norms, factors, near, line, far, squares,
     as00, as01, as02, as10, as11, as12, ar00, ar01, ar02, ar10, ar11, ar12,
     send0, send1, recv0, recv1, last0, last1, sum0, sum1, swap0, swap1, fin, acc, noise,
-    load_sem, gs_send, gs_recv, hp_send, hp_recv, gp_send, gp_recv, n_send, n_recv, f_send, f_recv, a_send, a_recv,
+    load_sem, gs_send, gs_recv, hp_send, hp_recv, gp_send, gp_recv, n_send, n_recv, f_send, f_recv, l_send, l_recv, a_send, a_recv,
     rs_send, rs_recv, last_send, last_recv, swap_send, swap_recv,
 ):
     gs, gp = (gs0, gs1, gs2), (gp0, gp1, gp2)
@@ -122,6 +124,7 @@
     for a, b in ((1, 0), (-1, 0), (0, 1), (0, -1)):
         others += [device_of(0, a, b), (chunk_of(0, a, b) * 2 + o, z)]
     barrier = pltpu.get_barrier_semaphore()
+    others += [device_of(0, 2, 0), device_of(0, 0, 2)]
     for device in others:
         pl.semaphore_signal(barrier, inc=1, device_id=device, device_id_type=MESH)
     pl.semaphore_wait(barrier, len(others))
@@ -201,11 +204,34 @@
             device_id=device_of(part, 1 - 2 * way, 0), device_id_type=MESH,
         )
 
+    def square(src, e):
+        def body(i, total):
+            x = src[pl.ds(pl.multiple_of(i * 64, 64), 64), :].astype(jnp.float32)
+            return total + fold(x * x)
+
+        total = lax.fori_loop(0, LEN // 64, body, jnp.zeros((8, 128), jnp.float32))
+        squares[e] = jnp.sqrt(jnp.broadcast_to(jnp.sum(total), (8, 128)))
+
+    def term_bound(j):
+        for e in range(2):
+            total = jnp.zeros((8, 128), jnp.float32)
+            for r in range(0, LEN, 128):
+                if e == 0:
+                    x = gs[j][r : r + 128, pl.ds(pl.multiple_of(c * PHASE_WIDTH[j], 128), PHASE_WIDTH[j])]
+                else:
+                    x = gp[j][r : r + 128, :]
+                x = x.astype(jnp.float32)
+                total = total + fold(x * x)
+            value = squares[e] * jnp.sqrt(jnp.broadcast_to(jnp.sum(total), (8, 128)))
+            row = TERM + 2 * j + e
+            factors[row : row + 1, :] = jnp.maximum(value, TINY)[0:1]
+
     def send_ahead(part, way, j):
         for k in range(2):
             for e in range(2):
                 value = term(e, part, j, chunk_of(part, 2, AHEAD[way][k]))
-                asend[part][j][way, k, e] = encode(value, AHEAD_SCALE)
+                row = TERM + 2 * j + e
+                asend[part][j][way, k, e] = encode(value, REACH / factors[row : row + 1, 0:1])
         ahead(part, way, j).start()
 
     for copy in g_loads:
@@ -241,12 +267,16 @@
 
     work = [(None, 0.3, functools.partial(lax.fori_loop, i, i + 1, act_gram, 0)) for i in range(4)]
     work += [(None, 0.4, functools.partial(transpose, hs, 0, i, i + 3)) for i in range(0, 18, 3)]
+    work += [(None, 0.5, functools.partial(square, hs, 0))]
     work += [(None, 0.1, functools.partial(wait_h))]
     work += [(None, 0.4, functools.partial(transpose, hp, 1, i, i + 3)) for i in range(0, 18, 3)]
+    work += [(None, 0.5, functools.partial(square, hp, 1))]
     later = []
     for j in range(3):
         here = (j, GATHER)
         terms_of = [(here, 0.1, functools.partial(wait_g, j))]
+        if j < 2:
+            terms_of += [(here, 0.2, functools.partial(term_bound, j))]
         terms_of += [(here, 0.5 - 0.1 * j, functools.partial(send_ahead, part, way, j)) for part, way in first]
         work += [
             ((j, need), 0.2, functools.partial(out_gram, j, lo, hi))
@@ -285,7 +315,7 @@
                 ready = steps >= whole.get(gate[0], steps) + 2
             else:
                 ready = gate is None or {(gate[0], k) for k in range(gate[1])} <= received
-                ready = ready and not (item.func in (send_ahead, prepare) and gate[0] not in taken)
+                ready = ready and not (item.func in (term_bound, send_ahead, prepare) and gate[0] not in taken)
             if ready and spare >= cost:
                 item()
                 spare -= cost
@@ -318,21 +348,45 @@
         for k in range(1, 8):
             total = total + norms[e, k]
         sq_norm = jnp.broadcast_to(jnp.sum(total), (8, 128))
-        factors[e] = jnp.minimum(1.0, bound / jnp.sqrt(sq_norm))
-        return jnp.max(factors[e])
-
-    f0, f1 = factor(0), factor(1)
+        value = jnp.minimum(1.0, bound / jnp.sqrt(sq_norm))
+        return value, value * jnp.sqrt(sq_norm)
+
+    (v0, m0), (v1, m1) = factor(0), factor(1)
+    factors[0:1, :] = v0[0:1]
+    factors[1:2, :] = v1[0:1]
+    factors[CHIP : CHIP + 1, :] = jnp.maximum(m0 + m1, TINY)[0:1]
+    f0, f1 = jnp.max(v0), jnp.max(v1)
     clip_ref[0] = f0
 
-    def give_factors(part, way):
-        return pltpu.make_async_remote_copy(
-            src_ref=factors, dst_ref=others_factors.at[part, way], send_sem=f_send.at[part, way],
-            recv_sem=f_recv.at[part, way], device_id=device_of(part, 1 - 2 * way, 0), device_id_type=MESH,
-        )
-
-
-    limit = 2.0 * bound
-    scale = [REACH / (limit * chips) for chips in (1, 1, 2, 2, 4, 8)]
+    def give_factors(part, k):
+        return pltpu.make_async_remote_copy(
+            src_ref=factors, dst_ref=near.at[part, k], send_sem=f_send.at[part, k], recv_sem=f_recv.at[part, k],
+            device_id=device_of(part, (1, -1, 2)[k], 0), device_id_type=MESH,
+        )
+
+    def give_line(part, k):
+        return pltpu.make_async_remote_copy(
+            src_ref=line.at[part], dst_ref=far.at[part, k], send_sem=l_send.at[part, k], recv_sem=l_recv.at[part, k],
+            device_id=device_of(part, 0, (1, -1, 2)[k]), device_id_type=MESH,
+        )
+
+    def near_bound(part, k):
+        return near[part, k, CHIP : CHIP + 1, 0:1]
+
+    def far_bound(part, k):
+        return far[part, k, 0:1, 0:1]
+
+    def sent_bound(part, way, slot):
+        if slot < 4:
+            own_bound = factors[CHIP : CHIP + 1, 0:1]
+            return own_bound if slot < 2 else own_bound + near_bound(part, way)
+        own_bound = line[part, 0:1, 0:1]
+        return own_bound if slot == 4 else own_bound + far_bound(part, way)
+
+    def got_bound(part, way, slot):
+        if slot < 4:
+            return near_bound(part, way) if slot < 2 else near_bound(part, way) + near_bound(part, 2)
+        return far_bound(part, way) if slot == 4 else far_bound(part, way) + far_bound(part, 2)
 
     def own(part, chunk, r):
         rows = pl.ds(pl.multiple_of(chunk * CHUNK + r, 16), STEP)
@@ -348,6 +402,7 @@
         lax.fori_loop(0, CHUNK // STEP, step, 0)
 
     def send_last_phase(part, way):
+        scale = REACH / sent_bound(part, way, 0)
         cols = slice(START[part] + PIECE_START[part][2], START[part] + WIDTH[part])
         for k in range(2):
             chunk = chunk_of(part, 2, AHEAD[way][k])
@@ -355,15 +410,17 @@
             def body(r, rows):
                 mine = pl.ds(pl.multiple_of(chunk * CHUNK + r, 16), STEP)
                 value = f0 * t[0, mine, cols] + f1 * t[1, mine, cols]
-                asend[part][2][way, k, 0, rows, :] = encode(value, scale[0])
+                asend[part][2][way, k, 0, rows, :] = encode(value, scale)
 
             over_rows(body)
         ahead(part, way, 2).start()
 
     for part in range(2):
         for way in range(2):
-            give_factors(part, way).start()
             send_last_phase(part, way)
+    for part in range(2):
+        for k in range(3):
+            give_factors(part, k).start()
 
     def message(part, way, slot):
         sign = 1 - 2 * way
@@ -386,22 +443,26 @@
             for j in range(3):
                 ahead(part, way, j).wait_recv()
         if slot >= 2:
-            their_f = [jnp.max(others_factors[part, way, e]) for e in range(2)]
+            their_f = [jnp.max(near[part, way, e : e + 1]) for e in range(2)]
+            unscale = near[part, way, :, 0:1] * (1.0 / REACH)
+        scale = REACH / sent_bound(part, way, slot)
 
         def body(r, rows):
             value = own(part, chunk_of(part, a, b), r)
             if slot < 2:
-                sends[part][way, slot, rows, :] = encode(value, scale[slot])
+                sends[part][way, slot, rows, :] = encode(value, scale)
                 return
             for j in range(3):
                 start = PIECE_START[part][j]
                 piece = value[:, start : start + PIECE_WIDTH[part][j]]
                 if j == 2:
-                    piece += decode(arecv[part][j][way, slot - 2, 0, rows, :], 1.0 / scale[0])
+                    piece += decode(arecv[part][j][way, slot - 2, 0, rows, :], unscale[CHIP : CHIP + 1])
                 else:
                     for e in range(2):
-                        piece += their_f[e] * decode(arecv[part][j][way, slot - 2, e, rows, :], 1.0 / AHEAD_SCALE)
-                sends[part][way, slot, rows, start : start + PIECE_WIDTH[part][j]] = encode(piece, scale[slot])
+                        row = TERM + 2 * j + e
+                        sent = arecv[part][j][way, slot - 2, e, rows, :]
+                        piece += decode(sent, unscale[row : row + 1] * their_f[e])
+                sends[part][way, slot, rows, start : start + PIECE_WIDTH[part][j]] = encode(piece, scale)
 
         over_rows(body)
         message(part, way, slot).start()
@@ -416,9 +477,10 @@
 
     def take(part, way, slot):
         message(part, way, slot).wait_recv()
+        unscale = got_bound(part, way, slot) * (1.0 / REACH)
 
         def body(r, rows):
-            sums[part][ORDER[way][slot], rows, :] += decode(recvs[part][way, slot, rows, :], 1.0 / scale[slot])
+            sums[part][ORDER[way][slot], rows, :] += decode(recvs[part][way, slot, rows, :], unscale)
 
         over_rows(body)
 
@@ -432,6 +494,14 @@
         for part in range(2):
             own_sum(part, b)
     both(first_phase, (2, 2))
+    for part in range(2):
+        give_factors(part, 2).wait_recv()
+        total = factors[CHIP : CHIP + 1, :]
+        for k in range(3):
+            total = total + near[part, k, CHIP : CHIP + 1, :]
+        line[part] = jnp.broadcast_to(total, (8, 128))
+        for k in range(3):
+            give_line(part, k).start()
     both(first_phase, (3, 1))
     for b in (3, 0):
         for part in range(2):
@@ -450,16 +520,18 @@
     for e, k in pairs:
         give_norm(e, k).wait_send()
     for part in range(2):
-        for way in range(2):
-            give_factors(part, way).wait_send()
+        for k in range(3):
+            give_factors(part, k).wait_send()
+            give_line(part, k).wait_send()
 
     both(take, (0, 0))
     both(take, (2, 2))
 
     for part in range(2):
+        scale = REACH / sent_bound(part, 0, 4)
 
         def body(r, rows):
-            value = encode(sums[part][2, rows, :], scale[4])
+            value = encode(sums[part][2, rows, :], scale)
             for way in range(2):
                 sends[part][way, 4, rows, :] = value
 
@@ -484,10 +556,13 @@
         b = 1 if way == 0 else 3
         rows = slice(0, TOP) if way == 0 else slice(TOP, CHUNK)
         message(part, way, 4).wait_recv()
-        sums[part][b, rows, :] += decode(recvs[part][way, 4, rows, :], 1.0 / scale[4])
+        give_line(part, way).wait_recv()
+        sums[part][b, rows, :] += decode(recvs[part][way, 4, rows, :], got_bound(part, way, 4) * (1.0 / REACH))
+
+        scale = REACH / sent_bound(part, way, 5)
 
         def body(r, rows):
-            sends[part][way, 5, rows, :] = encode(sums[part][b, rows, :], scale[5])
+            sends[part][way, 5, rows, :] = encode(sums[part][b, rows, :], scale)
 
         over_rows(body)
         for which in range(2):
@@ -512,6 +587,7 @@
     noise_load.wait()
     out_ref[...] = acc[...] + noise[...]
     for part in range(2):
+        give_line(part, 2).wait_recv()
         swap(part).wait_recv()
         for way in range(2):
             for slot in range(5):
@@ -524,7 +600,8 @@
                 last(part, way, which).wait_recv()
             value = sums[part][0, window(c), :] if which == 0 else swaps[part][...]
             for way in range(2):
-                value += decode(lasts[part][which, way], 1.0 / scale[5])
+                axes = part if which == 0 else 1 - part
+                value += decode(lasts[part][which, way], got_bound(axes, way, 5) * (1.0 / REACH))
             fin[which, :, cols] = value
     kept = pl.ds(pl.multiple_of(c * 8, 8), CHUNK // 2)
     for which in range(2):
@@ -563,8 +640,11 @@
             pltpu.VMEM((LEN, LEN), f32),
             pltpu.VMEM((8, 128), f32),
             pltpu.VMEM((2, 8, 8, 128), f32),
+            pltpu.VMEM((8, 128), f32),
+            pltpu.VMEM((2, 3, 8, 128), f32),
             pltpu.VMEM((2, 8, 128), f32),
-            pltpu.VMEM((2, 2, 2, 8, 128), f32),
+            pltpu.VMEM((2, 3, 8, 128), f32),
+            pltpu.VMEM((2, 8, 128), f32),
             *[pltpu.VMEM((2, 2, 2 - j // 2, CHUNK, part[j]), bf16) for part in PIECE_WIDTH for j in range(3)] * 2,
             pltpu.VMEM((2, 6, CHUNK, WIDTH[0]), bf16),
             pltpu.VMEM((2, 6, CHUNK, WIDTH[1]), bf16),
@@ -588,8 +668,10 @@
             dma((3, 5)),
             dma((2, 8)),
             dma((2, 8)),
-            dma((2, 2)),
-            dma((2, 2)),
+            dma((2, 3)),
+            dma((2, 3)),
+            dma((2, 3)),
+            dma((2, 3)),
             dma((2, 2, 3)),
             dma((2, 2, 3)),
             dma((2, 2, 5)),

time: 76 us -> 77.2 us (1.016)
  Pallas kernels: 71.5 us -> 72.7 us
    pallas_call x1, Pallas kernels: 71.5 us -> 72.7 us  [local(): pl.pallas_call(functools.partial(kernel, bound), out_shape=(jax.ShapeDtyp...]
where the time goes in v4:
time: 77.2 us; the launch traced here: 77 us
  Pallas kernels  72.7 us (94%)
  between operations  2.4 us (3%)
  local copies, waits for them, and re-layouts  1.97 us (3%)
    pallas_call x1, Pallas kernels, local(): pl.pallas_call(functools.partial(kernel, bound), out_shape=(jax.ShapeDtyp...  72.7 us
    unnamed x1, local copies, waits for them, and re-layouts  1.97 us

profile of v4, /device:TPU:1, one launch (start us, length us, event | category | flops | bytes accessed | tf_op | source)
XLA Modules:
  0.0 77.0 jit_solution(3808538388923352249)
XLA Ops:
  0.6 72.7 %shard_map.59 = (f32[72,2304]{1,0:T(8,128)}, f32[1]{0:T(128)}) custom-call(bf16[512,2304]{1,0:T(8,128)(2,1)} %h_hbm.1, bf16[64,2304]{1,0:T(8,128)(2,1)} %g_hbm.1, f32[72,2304]{1,0:T(8,128)} %acc_hbm.1, f32[72,2304]{1,0:T(8,128)} %noise_hbm.1), custom_call_target="tpu_custom_call" | custom-call | tf_op jit(solution)/shard_map/pallas_call | solution.py:628
  73.3 2.0 %copy.8 = f32[72,2304]{1,0:T(8,128)} copy(f32[72,2304]{1,0:T(8,128)} %get-tuple-element.4) | data formatting | bytes 1327104
